TPU v7x, 32 devices: a whole 2x2x4 slice. The times are simulated.
32 devices in a mesh: row: 4 (over z), col: 8 (over y, x, core).
Axes of the slice: x: 2, y: 2, z: 4, core: 2. Of those that a mesh axis runs over, the one named last changes fastest.
Arguments:
- factor_strip: float32 [4, 3, 512, 2048], P(None, None, 'col', 'row'), may hold values from -0.4375 to 0.4375
- pivots: float32 [3, 512], replicated, may hold values from 1 to 4
- right_side: float32 [4, 2048, 8192], P(None, 'row', 'col'), may hold values from -6 to 6
Outputs:
- solved: float32 [3, 512, 8192], P(None, None, 'col')
- trailing: float32 [4, 2048, 8192], P(None, 'row', 'col')
All inputs are finite; a program needn't handle non-finite values.
Results may differ from a plain program's by a relative error of at most 0.0001.
Values sent between devices are 32-bit elements; how exact they have to be, the bound alone decides.
A program may use at most 128 MiB of HBM per device.

v0:
```python
import jax
import jax.numpy as jnp
from jax import lax
from jax.sharding import PartitionSpec as P

PANELS = 3


def from_root(block, axis, source):
    block = jnp.where(lax.axis_index(axis) == source, block, jnp.zeros_like(block))
    return lax.psum(block, axis)


def per_device(factor_strip, pivots, right_side):
    row_index = lax.axis_index("row")
    row_count = lax.axis_size("row")
    sweeps = right_side.shape[0]
    block_ids = jnp.arange(sweeps, dtype=jnp.int32) * row_count + row_index
    gathered = lax.all_gather(factor_strip, "col", axis=2, tiled=True)
    work = right_side
    outputs = []
    for panel_index in range(PANELS):
        panel = gathered[:, panel_index]
        lower = jnp.tril(panel[0].T, -1) + jnp.diag(pivots[panel_index])
        local_solve = jax.scipy.linalg.solve_triangular(lower, work[0], lower=True)
        result = from_root(local_solve, "row", panel_index)
        outputs.append(result)
        update = jnp.einsum("bcr,cn->brn", panel, result, precision=lax.Precision.HIGHEST)
        keep = (block_ids > panel_index)[:, None, None]
        work = jnp.where(keep, work - update, work)
    return (jnp.stack(outputs), work)


def solution(mesh):
    return jax.shard_map(
        per_device,
        mesh=mesh,
        in_specs=(P(None, None, "col", "row"), P(), P(None, "row", "col")),
        out_specs=(P(None, None, "col"), P(None, "row", "col")),
        check_vma=False,
    )
```

profile of v0, /device:TPU:0, one launch (start us, length us, event | category | flops | bytes accessed | tf_op | source)
XLA Modules:
  0.0 511.2 jit_solution(17225175020078915204)
XLA Ops:
  7.2 2.7 copy.5
  10.0 1.7 slice_bitcast_fusion.14
  11.8 73.6 %all-gather.2.cloned.1.call-done = f32[4,3,512,512]{3,2,0,1:T(8,128)} async-done(((f32[4,3,64,512]{3,2,0,1:T(8,128)}), f32[4,3,512,512]{3,2,0,1:T(8,128)}) %all-gather.2.cloned.1.call-update) | async-done | bytes 12582928 | tf_op jit(solution)/shard_map/all_gather | solution.py:19
  85.3 3.7 fusion.35
  89.1 12.4 %while.6 = (s32[]{:T(128)}, f32[512,512]{0,1:T(8,128)}, s32[4,2]{0,1:T(2,128)S(1)}, f32[4,128,128]{2,1,0:T(8,128)S(1)}, s32[]{:T(128)}) while((s32[]{:T(128)}, f32[512,512]{0,1:T(8,128)}, s32[4,2]{0,1:T(2,128)S(1)}, f32[4,128,128]{2,1,0:T(8,128)S(1)}, s32[]{:T(128)}) %tuple.61), condition=%wide.while_cond, body=%wide.while_body.sunk | while | flops 2 | bytes 393321 | solution.py:25
  89.2 0.6 fusion.100
  89.8 2.3 dynamic-slice.17
  92.3 0.6 fusion.100
  92.9 2.3 dynamic-slice.17
  96.0 2.3 dynamic-slice.17
  98.5 0.6 fusion.100
  99.1 2.2 dynamic-slice.17
  101.5 0.7 copy-done.3
  102.2 40.1 %custom-call.5 = f32[4,128,128]{1,2,0:T(8,128)S(1)} custom-call(f32[4,128,128]{2,1,0:T(8,128)} %copy-done.3), custom_call_target="InvertDiagBlocksLowerTriangular" | custom-call | tf_op jit(solution)/shard_map/jit(_solve_triangular)/triangular_solve | solution.py:25
  142.3 0.6 fusion.55
  142.9 1.5 convolution_subtract_fusion.5
  144.4 0.6 fusion.74
  145.0 1.6 convolution_subtract_fusion.2
  146.7 0.6 fusion.72
  147.3 2.0 fusion.30
  149.4 0.6 fusion.71
  150.0 1.6 maximum_select_fusion
  151.8 8.7 %copy.11 = f32[4,512,1024]{1,2,0:T(8,128)} copy(f32[4,512,1024]{2,1,0:T(8,128)} %param.7) | data formatting | bytes 16777216 | tf_op args[2]
  160.5 12.4 %while.7 = (s32[]{:T(128)}, f32[512,512]{0,1:T(8,128)}, s32[4,2]{0,1:T(2,128)S(1)}, f32[4,128,128]{2,1,0:T(8,128)S(1)}, s32[]{:T(128)}) while((s32[]{:T(128)}, f32[512,512]{0,1:T(8,128)}, s32[4,2]{0,1:T(2,128)S(1)}, f32[4,128,128]{2,1,0:T(8,128)S(1)}, s32[]{:T(128)}) %tuple.78), condition=%wide.while_cond.clone, body=%wide.while_body.clone.sunk | while | flops 2 | bytes 393321 | solution.py:25
  160.6 0.6 fusion.101
  161.2 2.3 dynamic-slice.19
  164.3 2.3 dynamic-slice.19
  167.4 2.3 dynamic-slice.19
  170.5 2.2 dynamic-slice.19
  172.9 39.3 %custom-call.6 = f32[4,128,128]{1,2,0:T(8,128)S(1)} custom-call(f32[4,128,128]{2,1,0:T(8,128)S(1)} %get-tuple-element.24), custom_call_target="InvertDiagBlocksLowerTriangular" | custom-call | tf_op jit(solution)/shard_map/jit(_solve_triangular)/triangular_solve | solution.py:25
  212.2 25.9 %all-reduce.4.cloned.1.call-done = f32[512,1024]{1,0:T(8,128)} async-done(((f32[512,1024]{1,0:T(8,128)}), f32[512,1024]{1,0:T(8,128)}) %all-reduce.4.cloned.1.call-update) | async-done | bytes 2097168 | tf_op jit(solution)/shard_map/psum | solution.py:11
  238.1 18.9 %subtract_select_fusion.2 = f32[4,512,1024]{1,2,0:T(8,128)S(1)} fusion(f32[4,512,1024]{1,2,0:T(8,128)} %copy.11, pred[4]{0:T(512)(128)(4,1)S(1)} %broadcast_compare_fusion.2, f32[4,3,512,512]{3,2,0,1:T(8,128)} %all-gather.2.cloned.1.call-done, f32[512,1024]{1,0:T(8,128)} %all-reduce.4.cloned.1.call-done), kind=kOutput, calls=%fused_computation.8 | convolution fusion | flops 12889096192 | bytes 23068676 | tf_op jit(solution)/shard_map/bcr,cn->brn/dot_general | solution.py:28
  257.2 0.6 fusion.53
  257.9 1.9 convolution_subtract_fusion.4
  259.8 0.6 fusion.70
  260.5 2.7 convolution_subtract_fusion.1
  263.2 0.6 fusion.68
  263.9 3.7 fusion.27
  267.6 0.6 fusion.67
  268.3 1.6 maximum_select_fusion.1
  269.9 9.3 %while.8 = (s32[]{:T(128)}, f32[512,512]{0,1:T(8,128)S(1)}, s32[4,2]{0,1:T(2,128)S(1)}, f32[4,128,128]{2,1,0:T(8,128)S(1)}, s32[]{:T(128)}) while((s32[]{:T(128)}, f32[512,512]{0,1:T(8,128)S(1)}, s32[4,2]{0,1:T(2,128)S(1)}, f32[4,128,128]{2,1,0:T(8,128)S(1)}, s32[]{:T(128)}) %tuple.79), condition=%wide.while_cond.clone.1, body=%wide.while_body.clone.1.sunk | while | flops 2 | bytes 393321 | solution.py:25
  270.5 0.6 fusion.102
  271.1 1.4 dynamic-slice.21
  272.7 0.6 fusion.102
  273.3 1.4 dynamic-slice.21
  274.9 0.6 fusion.102
  275.5 1.4 dynamic-slice.21
  277.1 0.6 fusion.102
  277.7 1.4 dynamic-slice.21
  279.3 39.3 %custom-call.7 = f32[4,128,128]{1,2,0:T(8,128)S(1)} custom-call(f32[4,128,128]{2,1,0:T(8,128)S(1)} %get-tuple-element.25), custom_call_target="InvertDiagBlocksLowerTriangular" | custom-call | tf_op jit(solution)/shard_map/jit(_solve_triangular)/triangular_solve | solution.py:25
  318.6 36.9 %all-reduce.6.cloned.1.call-done = f32[512,1024]{1,0:T(8,128)} async-done(((f32[512,1024]{1,0:T(8,128)}), f32[512,1024]{1,0:T(8,128)}) %all-reduce.6.cloned.1.call-update) | async-done | bytes 2097168 | tf_op jit(solution)/shard_map/psum | solution.py:11
  355.5 18.9 %subtract_select_fusion.1 = f32[4,512,1024]{1,2,0:T(8,128)S(1)} fusion(f32[4,512,1024]{1,2,0:T(8,128)} %copy-done, pred[4]{0:T(512)(128)(4,1)S(1)} %broadcast_compare_fusion.1, f32[4,3,512,512]{3,2,0,1:T(8,128)} %all-gather.2.cloned.1.call-done, f32[512,1024]{1,0:T(8,128)} %all-reduce.6.cloned.1.call-done), kind=kOutput, calls=%fused_computation.7 | convolution fusion | flops 12889096192 | bytes 23068676 | tf_op jit(solution)/shard_map/bcr,cn->brn/dot_general | solution.py:28
  374.5 0.6 fusion.51
  375.2 1.0 convolution_subtract_fusion.3
  376.2 0.6 fusion.66
  376.9 1.8 convolution_subtract_fusion
  378.7 0.6 fusion.64
  379.4 2.8 fusion.24
  382.1 0.6 fusion.63
  382.8 1.6 maximum_select_fusion.2
  384.4 86.1 %all-reduce.8.cloned.1.call-done = f32[512,1024]{1,0:T(8,128)} async-done(((f32[512,1024]{1,0:T(8,128)}), f32[512,1024]{1,0:T(8,128)}) %all-reduce.8.cloned.1.call-update) | async-done | bytes 2097168 | tf_op jit(solution)/shard_map/psum | solution.py:11
  470.5 19.3 %subtract_select_fusion = f32[4,512,1024]{1,2,0:T(8,128)} fusion(f32[4,512,1024]{1,2,0:T(8,128)} %copy-done.1, pred[4]{0:T(512)(128)(4,1)S(1)} %broadcast_compare_fusion, f32[4,3,512,512]{3,2,0,1:T(8,128)} %all-gather.2.cloned.1.call-done, f32[512,1024]{1,0:T(8,128)} %all-reduce.8.cloned.1.call-done), kind=kOutput, calls=%fused_computation.6 | convolution fusion | flops 12889096192 | bytes 23068676 | tf_op jit(solution)/shard_map/bcr,cn->brn/dot_general | solution.py:28
  489.7 8.8 %copy.16 = f32[4,512,1024]{2,1,0:T(8,128)} copy(f32[4,512,1024]{1,2,0:T(8,128)} %subtract_select_fusion) | data formatting | bytes 16777216
  498.6 5.9 %pad_maximum_fusion = f32[3,512,1024]{2,1,0:T(8,128)} fusion(f32[1,512,1024]{2,1,0:T(8,128)} %bitcast.156, f32[1,512,1024]{2,1,0:T(8,128)} %bitcast.155, f32[1,512,1024]{2,1,0:T(8,128)S(1)} %bitcast.154), kind=kLoop, calls=%fused_computation.9 | loop fusion | flops 3145728 | bytes 12582912 | tf_op jit(solution)/shard_map/stack | solution.py:31
  (69 shorter events, 5.4 us)
Async XLA Ops:
  7.2 2.8 copy-start.4
  7.2 78.2 %all-gather.2.cloned.1.call-start = ((), (), s32[]{:S(2)}) async-start(), calls=%async_computation | async-start | bytes 14155776 | tf_op jit(solution)/shard_map/all_gather | solution.py:19
  9.9 228.2 %all-reduce.4.cloned.1.call-start = ((), (), s32[]{:S(2)}) async-start(), calls=%async_computation.1 | async-start | bytes 4194304 | tf_op jit(solution)/shard_map/psum | solution.py:11
  101.5 0.7 copy-start.3
  151.6 203.9 %all-reduce.6.cloned.1.call-start = ((), (), s32[]{:S(2)}) async-start(), calls=%async_computation.2 | async-start | bytes 4194304 | tf_op jit(solution)/shard_map/psum | solution.py:11
  257.0 10.6 %copy-start = (f32[4,512,1024]{1,2,0:T(8,128)}, f32[4,512,1024]{1,2,0:T(8,128)S(1)}, u32[]{:S(2)}) copy-start(f32[4,512,1024]{1,2,0:T(8,128)S(1)} %subtract_select_fusion.2) | copy-start | bytes 25165828
  269.8 200.6 %all-reduce.8.cloned.1.call-start = ((), (), s32[]{:S(2)}) async-start(), calls=%async_computation.3 | async-start | bytes 4194304 | tf_op jit(solution)/shard_map/psum | solution.py:11
  374.4 7.8 %copy-start.1 = (f32[4,512,1024]{1,2,0:T(8,128)}, f32[4,512,1024]{1,2,0:T(8,128)S(1)}, u32[]{:S(2)}) copy-start(f32[4,512,1024]{1,2,0:T(8,128)S(1)} %subtract_select_fusion.1) | copy-start | bytes 25165828
  489.7 8.8 %copy-start.2 = (f32[512,1024]{1,0:T(8,128)S(1)}, f32[512,1024]{1,0:T(8,128)}, u32[]{:S(2)}) copy-start(f32[512,1024]{1,0:T(8,128)} %all-reduce.4.cloned.1.call-done) | copy-start | bytes 6291460
Sparse Core Ops, SparseCore 0:
  10.5 74.8 all-gather.1
  151.7 86.3 all-reduce.3
  269.9 85.4 all-reduce.5
  384.5 85.9 all-reduce.7
where the time goes:
time: 518 us; the launch traced here: 511 us
  waiting for transfers between devices  223 us (43%)
  other arithmetic  133 us (26%)
  matrix products  83.9 us (16%)
  local copies, waits for them, and re-layouts  56.2 us (11%)
  between operations  14.4 us (3%)
    psum x3, waiting for transfers between devices, from_root(): return lax.psum(block, axis)  149 us
    another operation x5, other arithmetic, per_device(): local_solve = jax.scipy.linalg.solve_triangular(lower, work[0], lower=True)  122 us
    all_gather x1, waiting for transfers between devices, per_device(): gathered = lax.all_gather(factor_strip, 'col', axis=2, tiled=True)  73.6 us
    dot_general x3, matrix products, per_device(): jnp.einsum('bcr,cn->brn', panel, result, precision=lax.Precision.HIGHEST)  57.1 us
    another operation x64, local copies, waits for them, and re-layouts, per_device(): local_solve = jax.scipy.linalg.solve_triangular(lower, work[0], lower=True)  33.2 us
    another operation x21, matrix products, per_device(): local_solve = jax.scipy.linalg.solve_triangular(lower, work[0], lower=True)  26.8 us
    unnamed x13, local copies, waits for them, and re-layouts  20.9 us
  transfers between devices with their start and end apart: 4, of which 4 were waited for; matrix products, arithmetic and copies ran while one was open for 22% of the time, Pallas kernels for 0%

commit v1 on v0

v1 whole, which is shorter than its diff:
```python
import functools

import jax
import jax.numpy as jnp
from jax import lax
from jax.experimental import pallas as pl
from jax.experimental.pallas import tpu as pltpu
from jax.sharding import PartitionSpec as P

BLOCK = 128
BASE = 16
CHUNKS = 2
HIGHEST = lax.Precision.HIGHEST


def split(value):
    high = value.astype(jnp.bfloat16)
    low = (value - high.astype(jnp.float32)).astype(jnp.bfloat16)
    return high, low


def split_words(value):
    high = lax.reduce_precision(value, 8, 7)
    return high.astype(jnp.bfloat16), (value - high).astype(jnp.bfloat16)


def product(a_high, a_low, b_high, b_low):
    dot = functools.partial(jnp.dot, preferred_element_type=jnp.float32)
    return dot(a_high, b_high) + (dot(a_high, b_low) + dot(a_low, b_high))


def block_inverses(lower, diagonal):
    size = lower.shape[-1]
    mul = functools.partial(jnp.matmul, precision=HIGHEST)
    scaled = lower / diagonal[:, :, None]
    index = jnp.arange(size)
    eye = jnp.eye(size, dtype=jnp.float32)

    def same(width):
        return (index[:, None] // width) == (index[None, :] // width)

    power = jnp.where(same(BASE), -scaled, 0.0)
    inverse = eye + power
    width = 2
    while width < BASE:
        power = mul(power, power)
        inverse = inverse + mul(inverse, power)
        width *= 2
    width = BASE
    while width < size:
        off = jnp.where(same(2 * width) & ~same(width), scaled, 0.0)
        inverse = inverse - mul(mul(inverse, off), inverse)
        width *= 2
    return inverse / diagonal[:, None, :]


def chunk_kernel(panels, panel, row_count, tri_h, tri_l, inv_h, inv_l, rhs0, fac_h, fac_l, rhs, *rest):
    solved, trailing, x_high, x_low = rest[-4:]
    step = pl.program_id(0)
    total = panels * panel

    @pl.when(step == 0)
    def _():
        for i in range(total // BLOCK):
            lo, hi = i * BLOCK, (i + 1) * BLOCK
            p, at = lo // panel, lo % panel
            acc = rhs0[p, at:at + BLOCK, :]
            if i:
                acc = acc - product(tri_h[lo:hi, :lo], tri_l[lo:hi, :lo], x_high[:lo, :], x_low[:lo, :])
            a_high, a_low = split(acc)
            x = product(inv_h[i], inv_l[i], a_high, a_low)
            solved[p, at:at + BLOCK, :] = x
            b_high, b_low = split(x)
            x_high[lo:hi, :] = b_high
            x_low[lo:hi, :] = b_low

    @pl.when(step > 0)
    def _():
        trailing[0] = rhs[0] - product(fac_h[0], fac_l[0], x_high[...], x_low[...])


def chunk_call(index, chunks, tri, inv, rhs0, fac, right_side, row_count, previous):
    panels, panel = rhs0.shape[0], rhs0.shape[1]
    sweeps, rows, columns = right_side.shape
    width = columns // chunks
    total = panels * panel
    whole = lambda shape: pl.BlockSpec(shape, lambda s: (0,) * len(shape))
    sweep = lambda s: jnp.maximum(s - 1, 0)
    in_specs = [
        whole((total, total)), whole((total, total)),
        whole(inv[0].shape), whole(inv[1].shape),
        whole(rhs0.shape),
        pl.BlockSpec((1, rows, total), lambda s: (sweep(s), 0, 0)),
        pl.BlockSpec((1, rows, total), lambda s: (sweep(s), 0, 0)),
        pl.BlockSpec((1, rows, width), lambda s: (sweep(s), 0, index)),
    ]
    args = [*tri, *inv, rhs0, *fac, right_side]
    aliases = {}
    if previous is not None:
        in_specs += [pl.BlockSpec(memory_space=pl.ANY)] * 2
        aliases = {len(args): 0, len(args) + 1: 1}
        args += list(previous)
    return pl.pallas_call(
        functools.partial(chunk_kernel, panels, panel, row_count),
        grid=(sweeps + 1,),
        in_specs=in_specs,
        out_specs=[
            pl.BlockSpec((panels, panel, width), lambda s: (0, 0, index)),
            pl.BlockSpec((1, rows, width), lambda s: (sweep(s), 0, index)),
        ],
        out_shape=[
            jax.ShapeDtypeStruct((panels, panel, columns), jnp.float32),
            jax.ShapeDtypeStruct((sweeps, rows, columns), jnp.float32),
        ],
        scratch_shapes=[pltpu.VMEM((total, width), jnp.bfloat16)] * 2,
        input_output_aliases=aliases,
        compiler_params=pltpu.CompilerParams(vmem_limit_bytes=56 * 1024 * 1024),
        cost_estimate=pl.CostEstimate(
            flops=6 * (total * total // 2 + sweeps * rows * total) * width,
            bytes_accessed=4 * (total * total + sweeps * rows * total + 2 * sweeps * rows * width),
            transcendentals=0),
    )(*args)


def per_device(factor_strip, pivots, right_side):
    row_index = lax.axis_index("row")
    row_count = lax.axis_size("row")
    sweeps, rows, columns = right_side.shape
    panels, panel = pivots.shape
    total = panels * panel

    local = lax.all_gather(factor_strip[0], "row", axis=2, tiled=True)
    local = jnp.concatenate([local[p, :, p * panel:total] for p in range(panels)], axis=1)
    shared = lax.all_gather(local, "col", axis=0, tiled=True)
    gathered = lax.all_gather(factor_strip, "col", axis=2, tiled=True)
    width = columns // CHUNKS
    heads = [
        lax.all_gather(right_side[0, :, k * width:(k + 1) * width], "row", axis=0)[:panels]
        for k in range(CHUNKS)
    ]

    parts, at = [], 0
    for p in range(panels):
        tall = total - p * panel
        parts.append(jnp.pad(shared[:, at:at + tall].T, ((p * panel, 0), (0, 0))))
        at += tall
    full = jnp.concatenate(parts, axis=1)
    tri = split_words(full)
    blocks = jnp.stack([full[i:i + BLOCK, i:i + BLOCK] for i in range(0, total, BLOCK)])
    inv = split_words(block_inverses(jnp.tril(blocks, -1), pivots.reshape(-1, BLOCK)))

    block_ids = jnp.arange(sweeps, dtype=jnp.int32) * row_count + row_index
    keep = block_ids[:, None] > jnp.arange(panels, dtype=jnp.int32)[None, :]
    fac = jnp.where(keep[:, :, None, None], gathered, 0.0)
    fac = jnp.transpose(fac, (0, 3, 1, 2)).reshape(sweeps, rows, total)
    fac = split_words(fac)

    outs = None
    for k in range(CHUNKS):
        outs = chunk_call(k, CHUNKS, tri, inv, heads[k], fac, right_side, row_count, outs)
    return tuple(outs)


def solution(mesh):
    return jax.shard_map(
        per_device,
        mesh=mesh,
        in_specs=(P(None, None, "col", "row"), P(), P(None, "row", "col")),
        out_specs=(P(None, None, "col"), P(None, "row", "col")),
        check_vma=False,
    )
```

time: 518 us -> 427 us (0.82); the launches traced: 511 us -> 426 us
  other arithmetic: 133 us -> 28.4 us
  matrix products: 83.9 us -> 13.3 us
  Pallas kernels: 0 us -> 52.2 us
  waiting for transfers between devices: 223 us -> 268 us
  local copies, waits for them, and re-layouts: 56.2 us -> 50.1 us
    all_gather x0 -> x4, waiting for transfers between devices: none -> 233 us  [the longest x2 155 us: per_device(): lax.all_gather(right_side[0, :, k * width:(k + 1) * width], 'row', axis=0)]
    psum x3 -> x0, waiting for transfers between devices: 149 us -> none  [from_root(): return lax.psum(block, axis)]
    another operation x6 -> x0, other arithmetic: 128 us -> none  [the longest x5 122 us: per_device(): local_solve = jax.scipy.linalg.solve_triangular(lower, work[0], lower=True)]
    pallas_call x0 -> x2, Pallas kernels: none -> 52.2 us  [chunk_call(): pl.pallas_call(functools.partial(chunk_kernel, panels, panel, row_count),...]
    dot_general x3 -> x12, matrix products: 57.1 us -> 13.3 us  [the longest x6 7.3 us: block_inverses(): inverse = inverse - mul(mul(inverse, off), inverse)]
    all_gather x1, waiting for transfers between devices: 73.6 us -> 33.3 us  [per_device(): gathered = lax.all_gather(factor_strip, 'col', axis=2, tiled=True)]
    another operation x64 -> x1, local copies, waits for them, and re-layouts: 33.2 us -> 0.84 us  [per_device(): jnp.stack([full[i:i + BLOCK, i:i + BLOCK] for i in range(0, total, BLOCK)])]
    another operation x21 -> x0, matrix products: 26.8 us -> none  [per_device(): local_solve = jax.scipy.linalg.solve_triangular(lower, work[0], lower=True)]
  transfers between devices with their start and end apart: 4 -> 5, of which waited for: 4 -> 5; matrix products, arithmetic and copies ran while one was open for 22% -> 13% of each run, Pallas kernels for 0% -> 0%
where the time goes in v1:
time: 427 us; the launch traced here: 426 us
  waiting for transfers between devices  268 us (63%)
  Pallas kernels  52.2 us (12%)
  local copies, waits for them, and re-layouts  50.1 us (12%)
  other arithmetic  28.4 us (7%)
  between operations  14 us (3%)
  matrix products  13.3 us (3%)
    all_gather x2, waiting for transfers between devices, per_device(): lax.all_gather(right_side[0, :, k * width:(k + 1) * width], 'row', axis=0)  155 us
    pallas_call x2, Pallas kernels, chunk_call(): pl.pallas_call(functools.partial(chunk_kernel, panels, panel, row_count),...  52.2 us
    all_gather x1, waiting for transfers between devices, per_device(): shared = lax.all_gather(local, 'col', axis=0, tiled=True)  42 us
    all_gather x1, waiting for transfers between devices, per_device(): local = lax.all_gather(factor_strip[0], 'row', axis=2, tiled=True)  36.5 us
    all_gather x1, waiting for transfers between devices, per_device(): gathered = lax.all_gather(factor_strip, 'col', axis=2, tiled=True)  33.3 us
    convert_element_type x2, other arithmetic, split_words(): return (high.astype(jnp.bfloat16), (value - high).astype(jnp.bfloat16))  16.3 us
    unnamed x20, local copies, waits for them, and re-layouts  12.6 us
    reshape x1, local copies, waits for them, and re-layouts, per_device(): fac = jnp.transpose(fac, (0, 3, 1, 2)).reshape(sweeps, rows, total)  12.6 us
  transfers between devices with their start and end apart: 5, of which 5 were waited for; matrix products, arithmetic and copies ran while one was open for 13% of the time, Pallas kernels for 0%

profile of v1, /device:TPU:0, one launch (start us, length us, event | category | flops | bytes accessed | tf_op | source)
XLA Modules:
  0.0 425.8 jit_solution(13727018943435519950)
XLA Ops:
  7.2 0.0 all-gather.15.cloned.1.call-start
  7.2 1.8 slice.77
  9.0 0.0 copy-start.2
  9.0 0.0 all-gather.15.cloned.1.call-update
  9.0 0.0 all-gather.13.cloned.1.call-start
  9.1 3.0 fusion.44
  12.1 0.0 all-gather.13.cloned.1.call-update
  12.1 0.0 all-gather.9.cloned.1.call-start
  12.2 0.7 all-gather.9.cloned.1.call-update
  12.9 0.0 all-gather.7.cloned.1.call-start
  12.9 36.5 %all-gather.15.cloned.1.call-done = f32[1,3,64,2048]{3,2,1,0:T(8,128)} async-done(((f32[1,3,64,512]{3,2,1,0:T(8,128)}), f32[1,3,64,2048]{3,2,1,0:T(8,128)}) %all-gather.15.cloned.1.call-update) | async-done | bytes 1572880 | tf_op jit(solution)/shard_map/all_gather | solution.py:132
  49.4 0.9 slice_bitcast_fusion.2
  50.3 1.0 slice_bitcast_fusion.1
  51.3 1.0 slice_bitcast_fusion
  52.3 0.9 pad_maximum_fusion
  53.3 0.0 all-gather.7.cloned.1.call-update
  53.3 0.0 all-gather.11.cloned.1.call-start
  53.3 0.5 all-gather.11.cloned.1.call-update
  53.9 0.0 copy-done.2
  53.9 0.1 iota_compare_fusion.5
  54.0 0.1 fusion.37
  54.2 0.1 iota_compare_fusion.3
  54.2 76.9 %all-gather.13.cloned.1.call-done = f32[4,512,512]{2,1,0:T(8,128)} async-done(((f32[1,512,512]{2,1,0:T(8,128)}), f32[4,512,512]{2,1,0:T(8,128)}) %all-gather.13.cloned.1.call-update) | async-done | bytes 4194320 | tf_op jit(solution)/shard_map/all_gather | solution.py:138
  131.2 3.9 slice.119.rhs0
  135.1 77.6 %all-gather.9.cloned.1.call-done = f32[4,512,512]{2,1,0:T(8,128)} async-done(((f32[1,512,512]{2,1,0:T(8,128)}), f32[4,512,512]{2,1,0:T(8,128)}) %all-gather.9.cloned.1.call-update) | async-done | bytes 4194320 | tf_op jit(solution)/shard_map/all_gather | solution.py:138
  212.7 3.8 slice.118.rhs0
  216.5 42.0 %all-gather.7.cloned.1.call-done = f32[512,3072]{1,0:T(8,128)} async-done(((f32[64,3072]{1,0:T(8,128)}), f32[512,3072]{1,0:T(8,128)}) %all-gather.7.cloned.1.call-update) | async-done | bytes 6291472 | tf_op jit(solution)/shard_map/all_gather | solution.py:134
  258.5 1.3 slice.105
  259.8 1.3 copy.19
  261.1 3.8 slice.103
  264.9 2.4 copy.17
  267.3 3.5 slice.104
  270.8 2.9 copy.18
  273.8 0.8 fusion.31
  274.6 0.8 fusion.30
  275.5 0.8 fusion.29
  276.3 0.8 fusion.28
  277.2 0.8 fusion.27
  278.0 0.8 fusion.26
  278.9 0.8 fusion.25
  279.7 0.8 fusion.24
  280.5 1.3 fusion.12
  281.8 0.9 fusion.45
  282.7 0.9 fusion.46
  283.6 1.2 convolution_add_fusion.2
  284.8 0.9 convolution_add_fusion.1
  285.7 0.9 convolution_add_fusion
  286.6 1.1 fusion.9
  287.7 0.9 convolution_subtract_fusion.2
  288.6 0.0 copy-start
  288.6 0.0 copy-start.1
  288.6 1.1 fusion.7
  289.7 0.9 convolution_subtract_fusion.1
  290.7 1.1 fusion.5
  291.8 2.2 fusion.4
  294.0 0.0 copy-done
  294.0 0.0 copy-done.1
  294.0 5.1 %fusion.1 = (bf16[1536,1536]{1,0:T(8,128)(2,1)}, bf16[1536,1536]{1,0:T(8,128)(2,1)}) fusion(f32[512,512]{1,0:T(8,128)S(1)} %bitcast.94, f32[1024,512]{1,0:T(8,128)S(1)} %bitcast.89, f32[1536,512]{1,0:T(8,128)S(1)} %bitcast.84), kind=kLoop, calls=%fused_computation.7 | loop fusion | flops 28311552 | bytes 15728640 | tf_op jit(solution)/shard_map/convert_element_type | solution.py:24
  299.1 33.3 %all-gather.11.cloned.1.call-done = f32[4,3,512,512]{3,2,1,0:T(8,128)} async-done(((f32[4,3,64,512]{3,2,1,0:T(8,128)}), f32[4,3,512,512]{3,2,1,0:T(8,128)}) %all-gather.11.cloned.1.call-update) | async-done | bytes 12582928 | tf_op jit(solution)/shard_map/all_gather | solution.py:135
  332.4 10.8 %broadcast_select_fusion = f32[4,3,512,512]{3,2,1,0:T(8,128)} fusion(f32[4,3,512,512]{3,2,1,0:T(8,128)} %all-gather.11.cloned.1.call-done, pred[4,3]{1,0:T(4,128)(4,1)S(1)} %iota_compare_fusion.5), kind=kLoop, calls=%fused_computation.12 | loop fusion | flops 3145728 | bytes 25165836 | tf_op jit(solution)/shard_map/jit(_where)/select_n | solution.py:154
  343.2 12.6 %copy.15 = f32[4,512,1536]{2,1,0:T(8,128)} copy(f32[4,512,1536]{1,2,0:T(8,128)} %bitcast.79) | data formatting | bytes 25165824 | tf_op jit(solution)/shard_map/reshape | solution.py:155
  355.8 11.2 %fusion = (bf16[4,512,1536]{2,1,0:T(8,128)(2,1)}, bf16[4,512,1536]{2,1,0:T(8,128)(2,1)}) fusion(f32[4,512,1536]{2,1,0:T(8,128)} %copy.15), kind=kLoop, calls=%fused_computation.6 | loop fusion | flops 12582912 | bytes 25165824 | tf_op jit(solution)/shard_map/convert_element_type | solution.py:24
  367.0 26.0 %shard_map.50 = (f32[3,512,1024]{2,1,0:T(8,128)}, f32[4,512,1024]{2,1,0:T(8,128)}) custom-call(bf16[1536,1536]{1,0:T(8,128)(2,1)} %get-tuple-element.11.tri_h, bf16[1536,1536]{1,0:T(8,128)(2,1)} %get-tuple-element.10.tri_l, bf16[12,128,128]{2,1,0:T(8,128)(2,1)} %get-tuple-element.13.inv_h, bf16[12,128,128]{2,1,0:T(8,128)(2,1)} %get-tuple-element.12.inv_l, ...), custom_call_target="tpu_custom_call" | custom-call | flops 13287555072 | bytes 30408704 | tf_op jit(solution)/shard_map/pallas_call | solution.py:103
  393.0 26.2 %shard_map.51 = (f32[3,512,1024]{2,1,0:T(8,128)}, f32[4,512,1024]{2,1,0:T(8,128)}) custom-call(bf16[1536,1536]{1,0:T(8,128)(2,1)} %get-tuple-element.11.tri_h, bf16[1536,1536]{1,0:T(8,128)(2,1)} %get-tuple-element.10.tri_l, bf16[12,128,128]{2,1,0:T(8,128)(2,1)} %get-tuple-element.13.inv_h, ...), custom_call_target="tpu_custom_call", output_to_operand_aliasing={{0}: (8, {}), {1}: (9, {})} | custom-call | flops 13287555072 | bytes 30408704 | tf_op jit(solution)/shard_map/pallas_call | solution.py:103
  (9 shorter events, 0.1 us)
Async XLA Ops:
  7.2 42.2 %all-gather.15.cloned.1.call-start = ((), (), s32[]{:S(2)}) async-start(), calls=%async_computation.4 | async-start | bytes 1966080 | tf_op jit(solution)/shard_map/all_gather | solution.py:132
  9.0 44.9 %copy-start.2 = (f32[3,512]{1,0:T(4,128)S(1)}, f32[3,512]{1,0:T(4,128)}, u32[]{:S(2)}) copy-start(f32[3,512]{1,0:T(4,128)} %param.4) | copy-start | bytes 18436
  9.0 122.2 %all-gather.13.cloned.1.call-start = ((), (), s32[]{:S(2)}) async-start(), calls=%async_computation.3 | async-start | bytes 5242880 | tf_op jit(solution)/shard_map/all_gather | solution.py:138
  12.1 200.5 %all-gather.9.cloned.1.call-start = ((), (), s32[]{:S(2)}) async-start(), calls=%async_computation.1 | async-start | bytes 5242880 | tf_op jit(solution)/shard_map/all_gather | solution.py:138
  12.9 245.6 %all-gather.7.cloned.1.call-start = ((), (), s32[]{:S(2)}) async-start(), calls=%async_computation | async-start | bytes 7077888 | tf_op jit(solution)/shard_map/all_gather | solution.py:134
  53.3 279.1 %all-gather.11.cloned.1.call-start = ((), (), s32[]{:S(2)}) async-start(), calls=%async_computation.2 | async-start | bytes 14155776 | tf_op jit(solution)/shard_map/all_gather | solution.py:135
  288.6 5.4 %copy-start = (f32[512,1024]{0,1:T(8,128)S(1)}, f32[512,1024]{0,1:T(8,128)}, u32[]{:S(2)}) copy-start(f32[512,1024]{0,1:T(8,128)} %copy.18) | copy-start | bytes 6291460
  288.6 5.3 %copy-start.1 = (f32[512,512]{0,1:T(8,128)S(1)}, f32[512,512]{0,1:T(8,128)}, u32[]{:S(2)}) copy-start(f32[512,512]{0,1:T(8,128)} %copy.19) | copy-start | bytes 3145732
Sparse Core Ops, SparseCore 0:
  9.6 39.7 all-gather.14
  51.5 79.6 all-gather.12
  133.3 79.2 all-gather.8
  214.4 44.0 all-gather.6
  260.2 72.1 all-gather.10

commit v2 on v1

--- a/solution.py
+++ b/solution.py
@@ -122,6 +122,30 @@
     )(*args)
 
 
+def along_row(block, panels):
+    row_index = lax.axis_index("row")
+    row_count = lax.axis_size("row")
+    ahead, held = [], block
+    for step in range(row_count - 1):
+        pairs = [(r, r + 1) for r in range(row_count - 1) if 0 <= r - step < panels]
+        held = lax.ppermute(held, "row", pairs)
+        ahead.append(held)
+    back, held = [], block
+    for step in range(panels - 1):
+        pairs = [(r, r - 1) for r in range(1, row_count) if r + step < panels]
+        held = lax.ppermute(held, "row", pairs)
+        back.append(held)
+    found = []
+    for p in range(panels):
+        value = block
+        for r in range(row_count):
+            if r != p:
+                other = back[p - r - 1] if r < p else ahead[r - p - 1]
+                value = jnp.where(row_index == r, other, value)
+        found.append(value)
+    return found
+
+
 def per_device(factor_strip, pivots, right_side):
     row_index = lax.axis_index("row")
     row_count = lax.axis_size("row")
@@ -129,13 +153,14 @@
     panels, panel = pivots.shape
     total = panels * panel
 
-    local = lax.all_gather(factor_strip[0], "row", axis=2, tiled=True)
-    local = jnp.concatenate([local[p, :, p * panel:total] for p in range(panels)], axis=1)
+    shards = along_row(factor_strip[0], panels)
+    local = jnp.concatenate(
+        [shards[q][p] for p in range(panels) for q in range(p, panels)], axis=1)
+    gathered = lax.all_gather(factor_strip, "col", axis=2, tiled=True)
     shared = lax.all_gather(local, "col", axis=0, tiled=True)
-    gathered = lax.all_gather(factor_strip, "col", axis=2, tiled=True)
     width = columns // CHUNKS
     heads = [
-        lax.all_gather(right_side[0, :, k * width:(k + 1) * width], "row", axis=0)[:panels]
+        jnp.stack(along_row(right_side[0, :, k * width:(k + 1) * width], panels))
         for k in range(CHUNKS)
     ]
 
@@ -151,8 +176,8 @@
 
     block_ids = jnp.arange(sweeps, dtype=jnp.int32) * row_count + row_index
     keep = block_ids[:, None] > jnp.arange(panels, dtype=jnp.int32)[None, :]
-    fac = jnp.where(keep[:, :, None, None], gathered, 0.0)
-    fac = jnp.transpose(fac, (0, 3, 1, 2)).reshape(sweeps, rows, total)
+    fac = jnp.transpose(gathered, (0, 3, 1, 2)).reshape(sweeps, rows, total)
+    fac = jnp.where(jnp.repeat(keep, panel, axis=1)[:, None, :], fac, 0.0)
     fac = split_words(fac)
 
     outs = None

time: 427 us -> 312 us (0.73)
  the two profiles are of different devices: /device:TPU:0 before, /device:TPU:26 now
where the time goes in v2:
time: 312 us; the launch traced here: 311 us
  waiting for transfers between devices  147 us (47%)
  Pallas kernels  52.2 us (17%)
  local copies, waits for them, and re-layouts  38 us (12%)
  other arithmetic  26.8 us (9%)
  starting transfers between devices  18.8 us (6%)
  between operations  14.5 us (5%)
  matrix products  13.3 us (4%)
    ppermute x15, waiting for transfers between devices, along_row(): held = lax.ppermute(held, 'row', pairs)  147 us
    pallas_call x2, Pallas kernels, chunk_call(): pl.pallas_call(functools.partial(chunk_kernel, panels, panel, row_count),...  52.2 us
    ppermute x15, starting transfers between devices, along_row(): held = lax.ppermute(held, 'row', pairs)  18.7 us
    convert_element_type x2, other arithmetic, split_words(): return (high.astype(jnp.bfloat16), (value - high).astype(jnp.bfloat16))  15.7 us
    unnamed x26, local copies, waits for them, and re-layouts  13.5 us
    reshape x1, local copies, waits for them, and re-layouts, per_device(): fac = jnp.transpose(gathered, (0, 3, 1, 2)).reshape(sweeps, rows, total)  12.7 us
    another operation x4, other arithmetic, per_device(): jnp.stack(along_row(right_side[0, :, k * width:(k + 1) * width], panels))  9.55 us
    slice x3, local copies, waits for them, and re-layouts, per_device(): parts.append(jnp.pad(shared[:, at:at + tall].T, ((p * panel, 0), (0, 0))))  8.21 us
  transfers between devices with their start and end apart: 17, of which 9 were waited for; matrix products, arithmetic and copies ran while one was open for 17% of the time, Pallas kernels for 0%

profile of v2, /device:TPU:26, one launch (start us, length us, event | category | flops | bytes accessed | tf_op | source)
XLA Modules:
  0.0 311.1 jit_solution(6116360938648015774)
XLA Ops:
  7.2 1.0 slice_bitcast_fusion.2
  8.2 1.3 collective-permute-start
  9.5 0.7 collective-permute-start.3
  10.2 10.8 %collective-permute-done = f32[3,64,512]{2,1,0:T(8,128)S(1)} collective-permute-done((f32[3,64,512]{2,1,0:T(8,128)S(1)}, f32[3,64,512]{2,1,0:T(8,128)S(1)}, u32[]{:S(2)}, u32[]{:S(2)}) %collective-permute-start) | collective-permute-done | bytes 393248 | tf_op jit(solution)/shard_map/ppermute | solution.py:131
  21.0 1.3 collective-permute-start.1
  22.3 0.7 collective-permute-start.4
  23.0 9.9 %collective-permute-done.1 = f32[3,64,512]{2,1,0:T(8,128)S(1)} collective-permute-done((f32[3,64,512]{2,1,0:T(8,128)S(1)}, f32[3,64,512]{2,1,0:T(8,128)S(1)}, u32[]{:S(2)}, u32[]{:S(2)}) %collective-permute-start.1) | collective-permute-done | bytes 393248 | tf_op jit(solution)/shard_map/ppermute | solution.py:131
  32.9 1.3 collective-permute-start.2
  34.2 1.2 select_select_fusion
  35.4 8.4 %collective-permute-done.2 = f32[3,64,512]{2,1,0:T(8,128)S(1)} collective-permute-done((f32[3,64,512]{2,1,0:T(8,128)S(1)}, f32[3,64,512]{2,1,0:T(8,128)S(1)}, u32[]{:S(2)}, u32[]{:S(2)}) %collective-permute-start.2) | collective-permute-done | bytes 393248 | tf_op jit(solution)/shard_map/ppermute | solution.py:131
  43.9 0.9 copy-done.2
  44.9 0.7 all-gather.5.cloned.1.call-update
  45.6 1.7 slice_bitcast_fusion
  47.3 1.3 collective-permute-start.10
  48.6 1.3 collective-permute-start.5
  49.9 1.6 collective-permute-start.13
  51.5 23.8 %collective-permute-done.10 = f32[512,512]{1,0:T(8,128)S(1)} collective-permute-done((f32[512,512]{1,0:T(8,128)S(1)}, f32[512,512]{1,0:T(8,128)S(1)}, u32[]{:S(2)}, u32[]{:S(2)}) %collective-permute-start.10) | collective-permute-done | bytes 1048608 | tf_op jit(solution)/shard_map/ppermute | solution.py:131
  75.3 1.3 collective-permute-start.11
  76.6 0.7 collective-permute-start.8
  77.3 20.4 %collective-permute-done.5 = f32[512,512]{1,0:T(8,128)S(1)} collective-permute-done((f32[512,512]{1,0:T(8,128)S(1)}, f32[512,512]{1,0:T(8,128)S(1)}, u32[]{:S(2)}, u32[]{:S(2)}) %collective-permute-start.5) | collective-permute-done | bytes 1048608 | tf_op jit(solution)/shard_map/ppermute | solution.py:131
  97.8 1.3 collective-permute-start.6
  99.1 1.7 collective-permute-start.14
  100.8 19.6 %collective-permute-done.11 = f32[512,512]{1,0:T(8,128)} collective-permute-done((f32[512,512]{1,0:T(8,128)S(1)}, f32[512,512]{1,0:T(8,128)}, u32[]{:S(2)}, u32[]{:S(2)}) %collective-permute-start.11) | collective-permute-done | bytes 1048608 | tf_op jit(solution)/shard_map/ppermute | solution.py:131
  120.3 1.3 collective-permute-start.12
  121.8 1.7 collective-permute-start.9
  123.5 19.3 %collective-permute-done.6 = f32[512,512]{1,0:T(8,128)} collective-permute-done((f32[512,512]{1,0:T(8,128)S(1)}, f32[512,512]{1,0:T(8,128)}, u32[]{:S(2)}, u32[]{:S(2)}) %collective-permute-start.6) | collective-permute-done | bytes 1048608 | tf_op jit(solution)/shard_map/ppermute | solution.py:131
  142.8 1.3 collective-permute-start.7
  144.3 21.0 %collective-permute-done.12 = f32[512,512]{1,0:T(8,128)} collective-permute-done((f32[512,512]{1,0:T(8,128)}, f32[512,512]{1,0:T(8,128)}, u32[]{:S(2)}, u32[]{:S(2)}) %collective-permute-start.12) | collective-permute-done | bytes 1048608 | tf_op jit(solution)/shard_map/ppermute | solution.py:131
  165.3 3.0 select_bitcast_fusion.2
  168.3 2.0 pad_maximum_fusion.1.rhs0
  170.3 13.6 %collective-permute-done.7 = f32[512,512]{1,0:T(8,128)} collective-permute-done((f32[512,512]{1,0:T(8,128)}, f32[512,512]{1,0:T(8,128)}, u32[]{:S(2)}, u32[]{:S(2)}) %collective-permute-start.7) | collective-permute-done | bytes 1048608 | tf_op jit(solution)/shard_map/ppermute | solution.py:131
  183.8 2.7 select_bitcast_fusion.5
  186.5 1.9 pad_maximum_fusion.rhs0
  188.4 1.3 slice.115
  189.7 1.3 copy.17
  191.1 3.8 %slice.113 = f32[512,1536]{1,0:T(8,128)} slice(f32[512,3072]{1,0:T(8,128)} %all-gather.3.cloned.1.call-done), slice={[0:512], [0:1536]} | slice | bytes 6291456 | tf_op jit(solution)/shard_map/slice | solution.py:170
  194.8 2.4 copy.15
  197.2 3.2 %slice.114 = f32[512,1024]{1,0:T(8,128)} slice(f32[512,3072]{1,0:T(8,128)} %all-gather.3.cloned.1.call-done), slice={[0:512], [1536:2560]} | slice | bytes 4194304 | tf_op jit(solution)/shard_map/slice | solution.py:170
  200.4 2.9 copy.16
  203.3 0.8 fusion.38
  204.2 0.8 fusion.37
  205.0 0.8 fusion.36
  205.9 0.8 fusion.35
  206.7 0.8 fusion.34
  207.5 0.8 fusion.33
  208.4 0.8 fusion.32
  209.2 0.8 fusion.31
  210.1 1.3 fusion.12
  211.3 0.9 fusion.51
  212.2 0.9 fusion.52
  213.1 1.2 convolution_add_fusion.2
  214.3 0.9 convolution_add_fusion.1
  215.3 0.9 convolution_add_fusion
  216.2 1.1 fusion.9
  217.2 0.9 convolution_subtract_fusion.2
  218.2 1.1 fusion.7
  219.3 0.9 convolution_subtract_fusion.1
  220.2 1.1 fusion.5
  221.3 2.2 fusion.4
  223.5 4.8 %fusion.1 = (bf16[1536,1536]{1,0:T(8,128)(2,1)}, bf16[1536,1536]{1,0:T(8,128)(2,1)}) fusion(f32[512,512]{1,0:T(8,128)S(1)} %bitcast.146, f32[1024,512]{1,0:T(8,128)S(1)} %bitcast.141, f32[1536,512]{1,0:T(8,128)S(1)} %bitcast.135), kind=kLoop, calls=%fused_computation.7 | loop fusion | flops 28311552 | bytes 15728640 | tf_op jit(solution)/shard_map/convert_element_type | solution.py:24
  228.3 12.7 %copy.14 = f32[4,512,1536]{2,1,0:T(8,128)} copy(f32[4,512,1536]{1,2,0:T(8,128)} %bitcast.136) | data formatting | bytes 25165824 | tf_op jit(solution)/shard_map/reshape | solution.py:179
  241.0 11.0 %fusion = (bf16[4,512,1536]{2,1,0:T(8,128)(2,1)}, bf16[4,512,1536]{2,1,0:T(8,128)(2,1)}) fusion(f32[4,512,1536]{2,1,0:T(8,128)} %copy.14, pred[4,1536]{1,0:T(4,128)(4,1)S(1)} %bitcast.147), kind=kLoop, calls=%fused_computation.6 | loop fusion | flops 15728640 | bytes 25171968 | tf_op jit(solution)/shard_map/convert_element_type | solution.py:24
  252.0 26.0 %shard_map.50 = (f32[3,512,1024]{2,1,0:T(8,128)}, f32[4,512,1024]{2,1,0:T(8,128)}) custom-call(bf16[1536,1536]{1,0:T(8,128)(2,1)} %get-tuple-element.17.tri_h, bf16[1536,1536]{1,0:T(8,128)(2,1)} %get-tuple-element.16.tri_l, bf16[12,128,128]{2,1,0:T(8,128)(2,1)} %get-tuple-element.21.inv_h, bf16[12,128,128]{2,1,0:T(8,128)(2,1)} %get-tuple-element.20.inv_l, ...), custom_call_target="tpu_custom_call" | custom-call | flops 13287555072 | bytes 30408704 | tf_op jit(solution)/shard_map/pallas_call | solution.py:103
  278.0 26.2 %shard_map.51 = (f32[3,512,1024]{2,1,0:T(8,128)}, f32[4,512,1024]{2,1,0:T(8,128)}) custom-call(bf16[1536,1536]{1,0:T(8,128)(2,1)} %get-tuple-element.17.tri_h, bf16[1536,1536]{1,0:T(8,128)(2,1)} %get-tuple-element.16.tri_l, bf16[12,128,128]{2,1,0:T(8,128)(2,1)} %get-tuple-element.21.inv_h, ...), custom_call_target="tpu_custom_call", output_to_operand_aliasing={{0}: (8, {}), {1}: (9, {})} | custom-call | flops 13287555072 | bytes 30408704 | tf_op jit(solution)/shard_map/pallas_call | solution.py:103
  (37 shorter events, 0.6 us)
Async XLA Ops:
  7.2 181.3 %all-gather.3.cloned.1.call-start = ((), (), s32[]{:S(2)}) async-start(), calls=%async_computation | async-start | bytes 7077888 | tf_op jit(solution)/shard_map/all_gather | solution.py:160
  8.2 12.7 %collective-permute-start = (f32[3,64,512]{2,1,0:T(8,128)S(1)}, f32[3,64,512]{2,1,0:T(8,128)S(1)}, u32[]{:S(2)}, u32[]{:S(2)}) collective-permute-start(f32[3,64,512]{2,1,0:T(8,128)S(1)} %slice_bitcast_fusion.2), channel_id=1, source_target_pairs={{0,8},{8,16},{16,24},{1,9},{9,17},{17,25},{2,10},{10,18},{18,26},{... | collective-permute-start | bytes 1179656 | tf_op jit(solution)/shard_map/ppermute | solution.py:131
  9.5 12.7 %collective-permute-start.3 = (f32[3,64,512]{2,1,0:T(8,128)S(1)}, f32[3,64,512]{2,1,0:T(8,128)S(1)}, u32[]{:S(2)}, u32[]{:S(2)}) collective-permute-start(f32[3,64,512]{2,1,0:T(8,128)S(1)} %slice_bitcast_fusion.2), channel_id=1, source_target_pairs={{8,0},{16,8},{9,1},{17,9},{10,2},{18,10},{11,3},{19,11},{12,4},{20... | collective-permute-start | bytes 1179656 | tf_op jit(solution)/shard_map/ppermute | solution.py:136
  21.0 11.9 %collective-permute-start.1 = (f32[3,64,512]{2,1,0:T(8,128)S(1)}, f32[3,64,512]{2,1,0:T(8,128)S(1)}, u32[]{:S(2)}, u32[]{:S(2)}) collective-permute-start(f32[3,64,512]{2,1,0:T(8,128)S(1)} %collective-permute-done), channel_id=1, source_target_pairs={{8,16},{16,24},{9,17},{17,25},{10,18},{18,26},{11,19},{19,27},{12,... | collective-permute-start | bytes 1179656 | tf_op jit(solution)/shard_map/ppermute | solution.py:131
  22.3 11.9 %collective-permute-start.4 = (f32[3,64,512]{2,1,0:T(8,128)S(1)}, f32[3,64,512]{2,1,0:T(8,128)S(1)}, u32[]{:S(2)}, u32[]{:S(2)}) collective-permute-start(f32[3,64,512]{2,1,0:T(8,128)S(1)} %collective-permute-done.3), channel_id=1, source_target_pairs={{8,0},{9,1},{10,2},{11,3},{12,4},{13,5},{14,6},{15,7}} | collective-permute-start | bytes 1179656 | tf_op jit(solution)/shard_map/ppermute | solution.py:136
  32.9 10.9 %collective-permute-start.2 = (f32[3,64,512]{2,1,0:T(8,128)S(1)}, f32[3,64,512]{2,1,0:T(8,128)S(1)}, u32[]{:S(2)}, u32[]{:S(2)}) collective-permute-start(f32[3,64,512]{2,1,0:T(8,128)S(1)} %collective-permute-done.1), channel_id=1, source_target_pairs={{16,24},{17,25},{18,26},{19,27},{20,28},{21,29},{22,30},{23,31}} | collective-permute-start | bytes 1179656 | tf_op jit(solution)/shard_map/ppermute | solution.py:131
  35.4 108.7 %copy-start.3 = (f32[3,512]{1,0:T(4,128)S(1)}, f32[3,512]{1,0:T(4,128)}, u32[]{:S(2)}) copy-start(f32[3,512]{1,0:T(4,128)} %param.4) | copy-start | bytes 18436
  43.9 0.9 copy-start.2
  44.8 183.4 %all-gather.5.cloned.1.call-start = ((), (), s32[]{:S(2)}) async-start(), calls=%async_computation.1 | async-start | bytes 14155776 | tf_op jit(solution)/shard_map/all_gather | solution.py:159
  47.3 28.0 %collective-permute-start.10 = (f32[512,512]{1,0:T(8,128)S(1)}, f32[512,512]{1,0:T(8,128)S(1)}, u32[]{:S(2)}, u32[]{:S(2)}) collective-permute-start(f32[512,512]{1,0:T(8,128)S(1)} %get-tuple-element.14), channel_id=1, source_target_pairs={{0,8},{8,16},{16,24},{1,9},{9,17},{17,25},{2,10},{10,18},{18,26},{... | collective-permute-start | bytes 3145736 | tf_op jit(solution)/shard_map/ppermute | solution.py:131
  48.6 49.2 %collective-permute-start.5 = (f32[512,512]{1,0:T(8,128)S(1)}, f32[512,512]{1,0:T(8,128)S(1)}, u32[]{:S(2)}, u32[]{:S(2)}) collective-permute-start(f32[512,512]{1,0:T(8,128)S(1)} %get-tuple-element.15), channel_id=1, source_target_pairs={{0,8},{8,16},{16,24},{1,9},{9,17},{17,25},{2,10},{10,18},{18,26},{... | collective-permute-start | bytes 3145736 | tf_op jit(solution)/shard_map/ppermute | solution.py:131
  49.9 49.2 %collective-permute-start.13 = (f32[512,512]{1,0:T(8,128)S(1)}, f32[512,512]{1,0:T(8,128)}, u32[]{:S(2)}, u32[]{:S(2)}) collective-permute-start(f32[512,512]{1,0:T(8,128)S(1)} %get-tuple-element.14), channel_id=1, source_target_pairs={{8,0},{16,8},{9,1},{17,9},{10,2},{18,10},{11,3},{19,11},{12,4},{20... | collective-permute-start | bytes 3145736 | tf_op jit(solution)/shard_map/ppermute | solution.py:136
  75.3 45.0 %collective-permute-start.11 = (f32[512,512]{1,0:T(8,128)S(1)}, f32[512,512]{1,0:T(8,128)}, u32[]{:S(2)}, u32[]{:S(2)}) collective-permute-start(f32[512,512]{1,0:T(8,128)S(1)} %collective-permute-done.10), channel_id=1, source_target_pairs={{8,16},{16,24},{9,17},{17,25},{10,18},{18,26},{11,19},{19,27},{12,... | collective-permute-start | bytes 3145736 | tf_op jit(solution)/shard_map/ppermute | solution.py:131
  76.6 45.2 %collective-permute-start.8 = (f32[512,512]{1,0:T(8,128)S(1)}, f32[512,512]{1,0:T(8,128)S(1)}, u32[]{:S(2)}, u32[]{:S(2)}) collective-permute-start(f32[512,512]{1,0:T(8,128)S(1)} %get-tuple-element.15), channel_id=1, source_target_pairs={{8,0},{16,8},{9,1},{17,9},{10,2},{18,10},{11,3},{19,11},{12,4},{20... | collective-permute-start | bytes 3145736 | tf_op jit(solution)/shard_map/ppermute | solution.py:136
  97.8 45.0 %collective-permute-start.6 = (f32[512,512]{1,0:T(8,128)S(1)}, f32[512,512]{1,0:T(8,128)}, u32[]{:S(2)}, u32[]{:S(2)}) collective-permute-start(f32[512,512]{1,0:T(8,128)S(1)} %collective-permute-done.5), channel_id=1, source_target_pairs={{8,16},{16,24},{9,17},{17,25},{10,18},{18,26},{11,19},{19,27},{12,... | collective-permute-start | bytes 3145736 | tf_op jit(solution)/shard_map/ppermute | solution.py:131
  99.1 45.2 %collective-permute-start.14 = (f32[512,512]{1,0:T(8,128)}, f32[512,512]{1,0:T(8,128)}, u32[]{:S(2)}, u32[]{:S(2)}) collective-permute-start(f32[512,512]{1,0:T(8,128)} %collective-permute-done.13), channel_id=1, source_target_pairs={{8,0},{9,1},{10,2},{11,3},{12,4},{13,5},{14,6},{15,7}} | collective-permute-start | bytes 3145736 | tf_op jit(solution)/shard_map/ppermute | solution.py:136
  120.3 44.9 %collective-permute-start.12 = (f32[512,512]{1,0:T(8,128)}, f32[512,512]{1,0:T(8,128)}, u32[]{:S(2)}, u32[]{:S(2)}) collective-permute-start(f32[512,512]{1,0:T(8,128)} %collective-permute-done.11), channel_id=1, source_target_pairs={{16,24},{17,25},{18,26},{19,27},{20,28},{21,29},{22,30},{23,31}} | collective-permute-start | bytes 3145736 | tf_op jit(solution)/shard_map/ppermute | solution.py:131
  121.8 48.4 %collective-permute-start.9 = (f32[512,512]{1,0:T(8,128)S(1)}, f32[512,512]{1,0:T(8,128)}, u32[]{:S(2)}, u32[]{:S(2)}) collective-permute-start(f32[512,512]{1,0:T(8,128)S(1)} %collective-permute-done.8), channel_id=1, source_target_pairs={{8,0},{9,1},{10,2},{11,3},{12,4},{13,5},{14,6},{15,7}} | collective-permute-start | bytes 3145736 | tf_op jit(solution)/shard_map/ppermute | solution.py:136
  142.8 41.0 %collective-permute-start.7 = (f32[512,512]{1,0:T(8,128)}, f32[512,512]{1,0:T(8,128)}, u32[]{:S(2)}, u32[]{:S(2)}) collective-permute-start(f32[512,512]{1,0:T(8,128)} %collective-permute-done.6), channel_id=1, source_target_pairs={{16,24},{17,25},{18,26},{19,27},{20,28},{21,29},{22,30},{23,31}} | collective-permute-start | bytes 3145736 | tf_op jit(solution)/shard_map/ppermute | solution.py:131
  219.2 4.3 %copy-start = (f32[512,1024]{0,1:T(8,128)S(1)}, f32[512,1024]{0,1:T(8,128)}, u32[]{:S(2)}) copy-start(f32[512,1024]{0,1:T(8,128)} %copy.16) | copy-start | bytes 6291460
  219.2 4.3 %copy-start.1 = (f32[512,512]{0,1:T(8,128)S(1)}, f32[512,512]{0,1:T(8,128)}, u32[]{:S(2)}) copy-start(f32[512,512]{0,1:T(8,128)} %copy.17) | copy-start | bytes 3145732
Sparse Core Ops, SparseCore 0:
  45.0 46.4 all-gather.2
  93.4 72.1 all-gather.4
